TPU v7x, 512 devices: a whole 4x4x16 slice. The times are simulated.
512 devices in a mesh: af: 32 (over x, z_hi, core), gx: 4 (over z_lo), gy: 4 (over y).
Axes of the slice: x: 4, y: 4, z: 16 (z_hi: 4, z_lo: 4; z = z_hi * 4 + z_lo), core: 2. Of those that a mesh axis runs over, the one named last changes fastest.
Arguments:
- background: float32 [32, 2, 2, 3, 16, 32, 128], P('af', None, None, None, 'gx', 'gy'), may hold values from -6 to 6
- conductivity: float32 [3, 16, 32, 128], P(None, 'gx', 'gy'), may hold values from 0.1 to 1
- perturbation: float32 [3, 16, 32, 128], P(None, 'gx', 'gy'), may hold values from -15 to 15
- coupling: float32 [32], P('af'), may hold values from 0.3 to 3
- relaxation: float32 [2, 3], replicated, may hold values from 0.4 to 1.4
- receivers: int32 [1024], replicated, may hold values from 0 to 65535, as said below
- weights: float32 [32, 1024], P('af'), may hold values from 0.5 to 2
Outputs:
- hess_vec: float32 [3, 16, 32, 128], P(None, 'gx', 'gy', 'af')
Inputs may be any that keep to these rules, and one draw needn't show every extreme that they name: `receivers`: distinct flat cell indices (x 32 + y) * 128 + z of the whole grid.
All inputs are finite; a program needn't handle non-finite values.
Results may differ from a plain program's by a relative error of at most 0.0003.
Values sent between devices are 32-bit elements; how exact they have to be, the bound alone decides.
A program may use at most 64 MiB of HBM per device.

v0:
```python
import jax
import jax.numpy as jnp
from jax import lax
from jax.sharding import PartitionSpec as P


def extended_2(block, sides, width):
    for axis, dim in sides:
        count = lax.axis_size(axis)
        forward = [(i, i + 1) for i in range(count - 1)]
        backward = [(target, source) for source, target in forward]
        low = lax.ppermute(
            lax.slice_in_dim(block, block.shape[dim] - width, None, axis=dim), axis, forward
        )
        high = lax.ppermute(lax.slice_in_dim(block, 0, width, axis=dim), axis, backward)
        block = jnp.concatenate([low, block, high], axis=dim)
    return block


def curl_curl(padded):
    width_x = padded.shape[-3] - 2
    width_y = padded.shape[-2] - 2
    edge_x = padded[..., 0, :, :, :]
    edge_y = padded[..., 1, :, :, :]
    edge_z = padded[..., 2, :, :, :]

    def along_x(values):
        return (
            values[..., 1 : width_x + 2, : width_y + 1, :]
            - values[..., : width_x + 1, : width_y + 1, :]
        )

    def along_y(values):
        return (
            values[..., : width_x + 1, 1 : width_y + 2, :]
            - values[..., : width_x + 1, : width_y + 1, :]
        )

    def along_z(values):
        middle = values[..., : width_x + 1, : width_y + 1, :]
        raised = jnp.concatenate([middle[..., 1:], jnp.zeros_like(middle[..., :1])], axis=-1)
        return raised - middle

    face_x = along_y(edge_z) - along_z(edge_y)
    face_y = along_z(edge_x) - along_x(edge_z)
    face_z = along_x(edge_y) - along_y(edge_x)

    def back_x(values):
        return values[..., :width_x, 1:, :] - values[..., 1:, 1:, :]

    def back_y(values):
        return values[..., 1:, :width_y, :] - values[..., 1:, 1:, :]

    def back_z(values):
        middle = values[..., 1:, 1:, :]
        lowered = jnp.concatenate([jnp.zeros_like(middle[..., :1]), middle[..., :-1]], axis=-1)
        return lowered - middle

    curl_x = back_z(face_y) - back_y(face_z)
    curl_y = back_x(face_z) - back_z(face_x)
    curl_z = back_y(face_x) - back_x(face_y)
    return jnp.stack([curl_x, curl_y, curl_z], axis=-4)


def apply_operator(padded, fields, conductivity, coupled):
    curled = curl_curl(padded)
    damping = coupled * conductivity
    real_part = curled[..., 0, :, :, :, :] - damping * fields[..., 1, :, :, :, :]
    imag_part = curled[..., 1, :, :, :, :] + damping * fields[..., 0, :, :, :, :]
    return jnp.stack([real_part, imag_part], axis=-5)


def operate(fields, conductivity, coupled):
    padded = extended_2(fields, (("gx", 4), ("gy", 5)), 1)
    return apply_operator(padded, fields, conductivity, coupled)


def inner_sums(mapped, residual):
    mapped_real = mapped[..., 0, :, :, :, :]
    mapped_imag = mapped[..., 1, :, :, :, :]
    resid_real = residual[..., 0, :, :, :, :]
    resid_imag = residual[..., 1, :, :, :, :]
    axes_all = (-4, -3, -2, -1)
    dot_real = jnp.sum(mapped_real * resid_real + mapped_imag * resid_imag, axis=axes_all)
    dot_imag = jnp.sum(mapped_real * resid_imag - mapped_imag * resid_real, axis=axes_all)
    squares = jnp.sum(mapped_real * mapped_real + mapped_imag * mapped_imag, axis=axes_all)
    return lax.psum((dot_real, dot_imag, squares), ("gx", "gy"))


def complex_times(alpha_real, alpha_imag, fields):
    field_real = fields[..., 0, :, :, :, :]
    field_imag = fields[..., 1, :, :, :, :]
    real_part = alpha_real * field_real - alpha_imag * field_imag
    imag_part = alpha_real * field_imag + alpha_imag * field_real
    return jnp.stack([real_part, imag_part], axis=-5)


def relaxed_solve(source, coeffs, conductivity, coupled):
    answer = jnp.zeros_like(source)
    residual = source
    for turn_index in range(coeffs.shape[0]):
        mapped = operate(residual, conductivity, coupled)
        dot_real, dot_imag, squares = inner_sums(mapped, residual)
        factor = coeffs[turn_index] / (squares + 1e-06)
        alpha_real = (factor * dot_real)[..., None, None, None, None]
        alpha_imag = (factor * dot_imag)[..., None, None, None, None]
        answer = answer + complex_times(alpha_real, alpha_imag, residual)
        residual = residual - complex_times(alpha_real, alpha_imag, mapped)
    return answer


def station_cells(receivers, weights, width_x, width_y, layers):
    span_y = width_y * lax.axis_size("gy")
    plane_size = span_y * layers
    pos_x = receivers // plane_size - lax.axis_index("gx") * width_x
    pos_y = receivers // layers % span_y - lax.axis_index("gy") * width_y
    pos_z = receivers % layers
    inside = (pos_x >= 0) & (pos_x < width_x) & (pos_y >= 0) & (pos_y < width_y)
    cell_count = width_x * width_y * layers
    local_index = jnp.where(inside, (pos_x * width_y + pos_y) * layers + pos_z, cell_count)
    station_weight = (
        jnp.zeros((weights.shape[0], cell_count), jnp.float32)
        .at[:, local_index]
        .add(weights, mode="drop")
    )
    return station_weight.reshape(weights.shape[0], width_x, width_y, layers)


def polarization_term(field_bg, conductivity, perturbation, coupled, relaxation, station_mask):
    weighted = coupled * perturbation
    source = jnp.stack(
        [weighted * field_bg[..., 1, :, :, :, :], -(weighted * field_bg[..., 0, :, :, :, :])],
        axis=-5,
    )
    incremental = relaxed_solve(source, relaxation[0], conductivity, coupled)
    adjoint = relaxed_solve(incremental * station_mask, relaxation[1], conductivity, coupled)
    products = coupled * (
        field_bg[..., 0, :, :, :, :] * adjoint[..., 1, :, :, :, :]
        + field_bg[..., 1, :, :, :, :] * adjoint[..., 0, :, :, :, :]
    )
    return jnp.sum(products, axis=(0, 1))


def per_device(background, conductivity, perturbation, coupling, relaxation, receivers, weights):
    width_x = background.shape[4]
    width_y = background.shape[5]
    layers = background.shape[6]
    coupled = coupling.reshape(-1, 1, 1, 1, 1, 1)
    station_weight = station_cells(receivers, weights, width_x, width_y, layers)
    selector = jnp.array([1.0, 1.0, 0.0], jnp.float32)
    station_mask = (station_weight[:, None] * selector[None, :, None, None, None])[:, None, None]
    gradient_term = polarization_term(
        background, conductivity, perturbation, coupled, relaxation, station_mask
    )
    return lax.psum_scatter(gradient_term, "af", scatter_dimension=3, tiled=True)


def solution(mesh):
    placed = (
        P("af", None, None, None, "gx", "gy", None),
        P(None, "gx", "gy", None),
        P(None, "gx", "gy", None),
        P("af"),
        P(),
        P(),
        P("af", None),
    )
    return jax.shard_map(
        per_device, mesh=mesh, in_specs=placed, out_specs=P(None, "gx", "gy", "af"), check_vma=False
    )
```

profile of v0, /device:TPU:8, one launch (start us, length us, event | category | flops | bytes accessed | tf_op | source)
XLA Modules:
  0.0 534.5 jit_solution(4721874157151396263)
XLA Ops:
  2.9 4.5 collective-permute-start
  9.2 7.7 %collective-permute-start.3 = (f32[1,2,2,3,6,1,128]{6,5,4,3,1,2,0:T(1,128)S(1)}, f32[1,2,2,3,6,1,128]{6,5,4,3,1,2,0:T(1,128)S(1)}, u32[]{:S(2)}, u32[]{:S(2)}) collective-permute-start(f32[1,2,2,3,6,1,128]{6,5,4,3,1,2,0:T(1,128)S(1)} %get-tuple-element.98), channel_id=1, source_target_pairs={{1,0},{2,1},{3,2},{5,4},{6,5},{7,6},{9,8},{10,9},{11,10},{13,12},{... | collective-permute-start | bytes 110600 | tf_op jit(solution)/shard_map/ppermute | solution.py:15
  17.0 1.9 collective-permute-start.2
  19.6 3.3 collective-permute-done.2
  23.7 37.5 %all-reduce.30 = (f32[1,2]{1,0:T(1,128)S(1)}, f32[1,2]{1,0:T(1,128)S(1)}, f32[1,2]{1,0:T(1,128)S(1)}) all-reduce(f32[1,2]{1,0:T(1,128)S(1)} %bitcast.360, f32[1,2]{1,0:T(1,128)S(1)} %bitcast.359, f32[1,2]{1,0:T(1,128)S(1)} %bitcast.358), channel_id=1, replica_groups=mesh['af'=32,'gx'=4,'gy'=4] {'gx','gy'}, use_global_device_ids=true, to_apply=%region_1.2 | all-reduce | flops 6 | bytes 48 | tf_op jit(solution)/shard_map/psum | solution.py:87
  65.1 4.2 collective-permute-done.5
  69.4 5.1 collective-permute-start.7
  74.5 1.9 collective-permute-start.6
  76.4 3.9 collective-permute-done.6
  81.2 37.5 %all-reduce.29 = (f32[1,2]{1,0:T(1,128)S(1)}, f32[1,2]{1,0:T(1,128)S(1)}, f32[1,2]{1,0:T(1,128)S(1)}) all-reduce(f32[1,2]{1,0:T(1,128)S(1)} %bitcast.363, f32[1,2]{1,0:T(1,128)S(1)} %bitcast.362, f32[1,2]{1,0:T(1,128)S(1)} %bitcast.361), channel_id=1, replica_groups=mesh['af'=32,'gx'=4,'gy'=4] {'gx','gy'}, use_global_device_ids=true, to_apply=%region_7.8 | all-reduce | flops 6 | bytes 48 | tf_op jit(solution)/shard_map/psum | solution.py:87
  120.9 6.1 %scatter_custom_fusion = f32[4096]{0:T(1024)S(1)} fusion(s32[1024]{0:T(1024)S(1)} %compare_select_fusion, f32[1024]{0:T(1024)} %bitcast.376, f32[]{:T(128)} %constant.59.clone.1), kind=kCustom, calls=%fused_computation.288 | custom fusion | flops 1024 | bytes 16896 | tf_op jit(solution)/shard_map/scatter-add | solution.py:124
  128.4 4.6 collective-permute-done.9
  133.0 4.3 collective-permute-start.11
  137.3 1.9 collective-permute-start.10
  139.3 3.8 collective-permute-done.10
  144.0 37.5 %all-reduce.28 = (f32[1,2]{1,0:T(1,128)S(1)}, f32[1,2]{1,0:T(1,128)S(1)}, f32[1,2]{1,0:T(1,128)S(1)}) all-reduce(f32[1,2]{1,0:T(1,128)S(1)} %bitcast.366, f32[1,2]{1,0:T(1,128)S(1)} %bitcast.365, f32[1,2]{1,0:T(1,128)S(1)} %bitcast.364), channel_id=1, replica_groups=mesh['af'=32,'gx'=4,'gy'=4] {'gx','gy'}, use_global_device_ids=true, to_apply=%region_13.14 | all-reduce | flops 6 | bytes 48 | tf_op jit(solution)/shard_map/psum | solution.py:87
  185.5 4.2 collective-permute-done.13
  189.8 4.2 collective-permute-start.15
  194.0 1.9 collective-permute-start.14
  195.9 4.0 collective-permute-done.14
  200.7 37.4 %all-reduce.27 = (f32[1,2]{1,0:T(1,128)S(1)}, f32[1,2]{1,0:T(1,128)S(1)}, f32[1,2]{1,0:T(1,128)S(1)}) all-reduce(f32[1,2]{1,0:T(1,128)S(1)} %bitcast.369, f32[1,2]{1,0:T(1,128)S(1)} %bitcast.368, f32[1,2]{1,0:T(1,128)S(1)} %bitcast.367), channel_id=1, replica_groups=mesh['af'=32,'gx'=4,'gy'=4] {'gx','gy'}, use_global_device_ids=true, to_apply=%region_20.21 | all-reduce | flops 6 | bytes 48 | tf_op jit(solution)/shard_map/psum | solution.py:87
  242.1 4.2 collective-permute-done.17
  246.3 4.3 collective-permute-start.19
  250.6 1.9 collective-permute-start.18
  252.5 3.9 collective-permute-done.18
  257.3 37.5 %all-reduce.26 = (f32[1,2]{1,0:T(1,128)S(1)}, f32[1,2]{1,0:T(1,128)S(1)}, f32[1,2]{1,0:T(1,128)S(1)}) all-reduce(f32[1,2]{1,0:T(1,128)S(1)} %bitcast.372, f32[1,2]{1,0:T(1,128)S(1)} %bitcast.371, f32[1,2]{1,0:T(1,128)S(1)} %bitcast.370), channel_id=1, replica_groups=mesh['af'=32,'gx'=4,'gy'=4] {'gx','gy'}, use_global_device_ids=true, to_apply=%region_26.27 | all-reduce | flops 6 | bytes 48 | tf_op jit(solution)/shard_map/psum | solution.py:87
  297.0 4.5 collective-permute-start.20
  303.3 4.2 collective-permute-start.23
  307.6 1.9 collective-permute-start.22
  311.4 2.0 collective-permute-done.22
  314.4 37.8 %all-reduce.25 = (f32[1,2]{1,0:T(1,128)S(1)}, f32[1,2]{1,0:T(1,128)S(1)}, f32[1,2]{1,0:T(1,128)S(1)}) all-reduce(f32[1,2]{1,0:T(1,128)S(1)} %bitcast.373, f32[1,2]{1,0:T(1,128)S(1)} %bitcast.375, f32[1,2]{1,0:T(1,128)S(1)} %bitcast.374), channel_id=1, replica_groups=mesh['af'=32,'gx'=4,'gy'=4] {'gx','gy'}, use_global_device_ids=true, to_apply=%region_32.33 | all-reduce | flops 6 | bytes 48 | tf_op jit(solution)/shard_map/psum | solution.py:87
  353.3 180.6 %all-reduce.24 = f32[3,4,8,128]{2,3,1,0:T(8,128)S(1)} all-reduce(f32[3,4,8,128]{2,3,1,0:T(8,128)S(1)} %copy.127), channel_id=2, replica_groups=mesh['af'=32,'gx'=4,'gy'=4] {'af'}, use_global_device_ids=true, to_apply=%region_38.39.clone | all-reduce | flops 12288 | bytes 98304
  (164 shorter events, 31.6 us)
Async XLA Ops:
  0.0 1.5 copy-start
  1.6 6.0 %collective-permute-start.1 = (f32[1,2,2,3,1,8,128]{6,5,4,3,1,2,0:T(8,128)S(1)}, f32[1,2,2,3,1,8,128]{6,5,4,3,1,2,0:T(8,128)S(1)}, u32[]{:S(2)}, u32[]{:S(2)}) collective-permute-start(f32[1,2,2,3,1,8,128]{6,5,4,3,1,2,0:T(8,128)S(1)} %get-tuple-element.145), channel_id=1, source_target_pairs={{4,0},{8,4},{12,8},{5,1},{9,5},{13,9},{6,2},{10,6},{14,10},{7,3},{... | collective-permute-start | bytes 147464 | tf_op jit(solution)/shard_map/ppermute | solution.py:15
  2.9 6.3 %collective-permute-start = (f32[1,2,2,3,1,8,128]{6,5,4,3,1,2,0:T(8,128)S(1)}, f32[1,2,2,3,1,8,128]{6,5,4,3,1,2,0:T(8,128)S(1)}, u32[]{:S(2)}, u32[]{:S(2)}) collective-permute-start(f32[1,2,2,3,1,8,128]{6,5,4,3,1,2,0:T(8,128)S(1)} %get-tuple-element.144), channel_id=1, source_target_pairs={{0,4},{4,8},{8,12},{1,5},{5,9},{9,13},{2,6},{6,10},{10,14},{3,7},{... | collective-permute-start | bytes 147464 | tf_op jit(solution)/shard_map/ppermute | solution.py:12
  9.2 9.7 %copy-start.1 = (f32[2,3]{1,0:T(2,128)S(1)}, f32[2,3]{1,0:T(2,128)}, u32[]{:S(2)}) copy-start(f32[2,3]{1,0:T(2,128)} %param.12) | copy-start | bytes 76
  9.2 10.3 %collective-permute-start.3 = (f32[1,2,2,3,6,1,128]{6,5,4,3,1,2,0:T(1,128)S(1)}, f32[1,2,2,3,6,1,128]{6,5,4,3,1,2,0:T(1,128)S(1)}, u32[]{:S(2)}, u32[]{:S(2)}) collective-permute-start(f32[1,2,2,3,6,1,128]{6,5,4,3,1,2,0:T(1,128)S(1)} %get-tuple-element.98), channel_id=1, source_target_pairs={{1,0},{2,1},{3,2},{5,4},{6,5},{7,6},{9,8},{10,9},{11,10},{13,12},{... | collective-permute-start | bytes 110600 | tf_op jit(solution)/shard_map/ppermute | solution.py:15
  17.0 5.9 %collective-permute-start.2 = (f32[1,2,2,3,6,1,128]{6,5,4,3,1,2,0:T(1,128)S(1)}, f32[1,2,2,3,6,1,128]{6,5,4,3,1,2,0:T(1,128)S(1)}, u32[]{:S(2)}, u32[]{:S(2)}) collective-permute-start(f32[1,2,2,3,6,1,128]{6,5,4,3,1,2,0:T(1,128)S(1)} %get-tuple-element.97), channel_id=1, source_target_pairs={{0,1},{1,2},{2,3},{4,5},{5,6},{6,7},{8,9},{9,10},{10,11},{12,13},{... | collective-permute-start | bytes 110600 | tf_op jit(solution)/shard_map/ppermute | solution.py:12
  62.0 3.0 collective-permute-start.4
  63.3 6.0 %collective-permute-start.5 = (f32[1,2,2,3,1,8,128]{6,5,4,1,2,3,0:T(8,128)S(1)}, f32[1,2,2,3,1,8,128]{6,5,4,1,2,3,0:T(8,128)S(1)}, u32[]{:S(2)}, u32[]{:S(2)}) collective-permute-start(f32[1,2,2,3,1,8,128]{6,5,4,1,2,3,0:T(8,128)S(1)} %copy.178), channel_id=1, source_target_pairs={{4,0},{8,4},{12,8},{5,1},{9,5},{13,9},{6,2},{10,6},{14,10},{7,3},{... | collective-permute-start | bytes 147464 | tf_op jit(solution)/shard_map/ppermute | solution.py:15
  69.4 7.1 %collective-permute-start.7 = (f32[1,2,2,3,6,1,128]{6,5,4,1,2,3,0:T(1,128)S(1)}, f32[1,2,2,3,6,1,128]{6,5,4,1,2,3,0:T(1,128)S(1)}, u32[]{:S(2)}, u32[]{:S(2)}) collective-permute-start(f32[1,2,2,3,6,1,128]{6,5,4,1,2,3,0:T(1,128)S(1)} %get-tuple-element.96), channel_id=1, source_target_pairs={{1,0},{2,1},{3,2},{5,4},{6,5},{7,6},{9,8},{10,9},{11,10},{13,12},{... | collective-permute-start | bytes 110600 | tf_op jit(solution)/shard_map/ppermute | solution.py:15
  74.5 5.9 %collective-permute-start.6 = (f32[1,2,2,3,6,1,128]{6,5,4,1,2,3,0:T(1,128)S(1)}, f32[1,2,2,3,6,1,128]{6,5,4,1,2,3,0:T(1,128)S(1)}, u32[]{:S(2)}, u32[]{:S(2)}) collective-permute-start(f32[1,2,2,3,6,1,128]{6,5,4,1,2,3,0:T(1,128)S(1)} %get-tuple-element.95), channel_id=1, source_target_pairs={{0,1},{1,2},{2,3},{4,5},{5,6},{6,7},{8,9},{9,10},{10,11},{12,13},{... | collective-permute-start | bytes 110600 | tf_op jit(solution)/shard_map/ppermute | solution.py:12
  119.5 1.3 copy-start.2
  119.5 8.7 %collective-permute-start.8 = (f32[1,2,2,3,1,8,128]{6,5,4,1,2,3,0:T(8,128)S(1)}, f32[1,2,2,3,1,8,128]{6,5,4,1,2,3,0:T(8,128)S(1)}, u32[]{:S(2)}, u32[]{:S(2)}) collective-permute-start(f32[1,2,2,3,1,8,128]{6,5,4,1,2,3,0:T(8,128)S(1)} %copy.179), channel_id=1, source_target_pairs={{0,4},{4,8},{8,12},{1,5},{5,9},{9,13},{2,6},{6,10},{10,14},{3,7},{... | collective-permute-start | bytes 147464 | tf_op jit(solution)/shard_map/ppermute | solution.py:12
  127.0 6.0 %collective-permute-start.9 = (f32[1,2,2,3,1,8,128]{6,5,4,1,2,3,0:T(8,128)S(1)}, f32[1,2,2,3,1,8,128]{6,5,4,1,2,3,0:T(8,128)S(1)}, u32[]{:S(2)}, u32[]{:S(2)}) collective-permute-start(f32[1,2,2,3,1,8,128]{6,5,4,1,2,3,0:T(8,128)S(1)} %copy.180), channel_id=1, source_target_pairs={{4,0},{8,4},{12,8},{5,1},{9,5},{13,9},{6,2},{10,6},{14,10},{7,3},{... | collective-permute-start | bytes 147464 | tf_op jit(solution)/shard_map/ppermute | solution.py:15
  133.0 6.3 %collective-permute-start.11 = (f32[1,2,2,3,6,1,128]{6,5,4,1,2,3,0:T(1,128)S(1)}, f32[1,2,2,3,6,1,128]{6,5,4,1,2,3,0:T(1,128)S(1)}, u32[]{:S(2)}, u32[]{:S(2)}) collective-permute-start(f32[1,2,2,3,6,1,128]{6,5,4,1,2,3,0:T(1,128)S(1)} %get-tuple-element.94), channel_id=1, source_target_pairs={{1,0},{2,1},{3,2},{5,4},{6,5},{7,6},{9,8},{10,9},{11,10},{13,12},{... | collective-permute-start | bytes 110600 | tf_op jit(solution)/shard_map/ppermute | solution.py:15
  137.3 1.9 copy-start.3
  137.3 5.9 %collective-permute-start.10 = (f32[1,2,2,3,6,1,128]{6,5,4,1,2,3,0:T(1,128)S(1)}, f32[1,2,2,3,6,1,128]{6,5,4,1,2,3,0:T(1,128)S(1)}, u32[]{:S(2)}, u32[]{:S(2)}) collective-permute-start(f32[1,2,2,3,6,1,128]{6,5,4,1,2,3,0:T(1,128)S(1)} %get-tuple-element.93), channel_id=1, source_target_pairs={{0,1},{1,2},{2,3},{4,5},{5,6},{6,7},{8,9},{9,10},{10,11},{12,13},{... | collective-permute-start | bytes 110600 | tf_op jit(solution)/shard_map/ppermute | solution.py:12
  182.4 3.0 collective-permute-start.12
  183.7 6.0 %collective-permute-start.13 = (f32[1,2,2,3,1,8,128]{6,5,4,1,2,3,0:T(8,128)S(1)}, f32[1,2,2,3,1,8,128]{6,5,4,1,2,3,0:T(8,128)S(1)}, u32[]{:S(2)}, u32[]{:S(2)}) collective-permute-start(f32[1,2,2,3,1,8,128]{6,5,4,1,2,3,0:T(8,128)S(1)} %copy.182), channel_id=1, source_target_pairs={{4,0},{8,4},{12,8},{5,1},{9,5},{13,9},{6,2},{10,6},{14,10},{7,3},{... | collective-permute-start | bytes 147464 | tf_op jit(solution)/shard_map/ppermute | solution.py:15
  189.8 6.1 %collective-permute-start.15 = (f32[1,2,2,3,6,1,128]{6,5,4,1,2,3,0:T(1,128)S(1)}, f32[1,2,2,3,6,1,128]{6,5,4,1,2,3,0:T(1,128)S(1)}, u32[]{:S(2)}, u32[]{:S(2)}) collective-permute-start(f32[1,2,2,3,6,1,128]{6,5,4,1,2,3,0:T(1,128)S(1)} %get-tuple-element.92), channel_id=1, source_target_pairs={{1,0},{2,1},{3,2},{5,4},{6,5},{7,6},{9,8},{10,9},{11,10},{13,12},{... | collective-permute-start | bytes 110600 | tf_op jit(solution)/shard_map/ppermute | solution.py:15
  194.0 5.9 %collective-permute-start.14 = (f32[1,2,2,3,6,1,128]{6,5,4,1,2,3,0:T(1,128)S(1)}, f32[1,2,2,3,6,1,128]{6,5,4,1,2,3,0:T(1,128)S(1)}, u32[]{:S(2)}, u32[]{:S(2)}) collective-permute-start(f32[1,2,2,3,6,1,128]{6,5,4,1,2,3,0:T(1,128)S(1)} %get-tuple-element.91), channel_id=1, source_target_pairs={{0,1},{1,2},{2,3},{4,5},{5,6},{6,7},{8,9},{9,10},{10,11},{12,13},{... | collective-permute-start | bytes 110600 | tf_op jit(solution)/shard_map/ppermute | solution.py:12
  239.0 3.0 collective-permute-start.16
  240.3 6.0 %collective-permute-start.17 = (f32[1,2,2,3,1,8,128]{6,5,4,1,2,3,0:T(8,128)S(1)}, f32[1,2,2,3,1,8,128]{6,5,4,1,2,3,0:T(8,128)S(1)}, u32[]{:S(2)}, u32[]{:S(2)}) collective-permute-start(f32[1,2,2,3,1,8,128]{6,5,4,1,2,3,0:T(8,128)S(1)} %copy.184), channel_id=1, source_target_pairs={{4,0},{8,4},{12,8},{5,1},{9,5},{13,9},{6,2},{10,6},{14,10},{7,3},{... | collective-permute-start | bytes 147464 | tf_op jit(solution)/shard_map/ppermute | solution.py:15
  246.3 6.2 %collective-permute-start.19 = (f32[1,2,2,3,6,1,128]{6,5,4,1,2,3,0:T(1,128)S(1)}, f32[1,2,2,3,6,1,128]{6,5,4,1,2,3,0:T(1,128)S(1)}, u32[]{:S(2)}, u32[]{:S(2)}) collective-permute-start(f32[1,2,2,3,6,1,128]{6,5,4,1,2,3,0:T(1,128)S(1)} %get-tuple-element.90), channel_id=1, source_target_pairs={{1,0},{2,1},{3,2},{5,4},{6,5},{7,6},{9,8},{10,9},{11,10},{13,12},{... | collective-permute-start | bytes 110600 | tf_op jit(solution)/shard_map/ppermute | solution.py:15
  250.6 5.9 %collective-permute-start.18 = (f32[1,2,2,3,6,1,128]{6,5,4,1,2,3,0:T(1,128)S(1)}, f32[1,2,2,3,6,1,128]{6,5,4,1,2,3,0:T(1,128)S(1)}, u32[]{:S(2)}, u32[]{:S(2)}) collective-permute-start(f32[1,2,2,3,6,1,128]{6,5,4,1,2,3,0:T(1,128)S(1)} %get-tuple-element.89), channel_id=1, source_target_pairs={{0,1},{1,2},{2,3},{4,5},{5,6},{6,7},{8,9},{9,10},{10,11},{12,13},{... | collective-permute-start | bytes 110600 | tf_op jit(solution)/shard_map/ppermute | solution.py:12
  295.7 6.0 %collective-permute-start.21 = (f32[1,2,2,3,1,8,128]{6,5,4,3,1,2,0:T(8,128)S(1)}, f32[1,2,2,3,1,8,128]{6,5,4,3,1,2,0:T(8,128)S(1)}, u32[]{:S(2)}, u32[]{:S(2)}) collective-permute-start(f32[1,2,2,3,1,8,128]{6,5,4,3,1,2,0:T(8,128)S(1)} %get-tuple-element.117), channel_id=1, source_target_pairs={{4,0},{8,4},{12,8},{5,1},{9,5},{13,9},{6,2},{10,6},{14,10},{7,3},{... | collective-permute-start | bytes 147464 | tf_op jit(solution)/shard_map/ppermute | solution.py:15
  297.0 6.3 %collective-permute-start.20 = (f32[1,2,2,3,1,8,128]{6,5,4,3,1,2,0:T(8,128)S(1)}, f32[1,2,2,3,1,8,128]{6,5,4,3,1,2,0:T(8,128)S(1)}, u32[]{:S(2)}, u32[]{:S(2)}) collective-permute-start(f32[1,2,2,3,1,8,128]{6,5,4,3,1,2,0:T(8,128)S(1)} %get-tuple-element.116), channel_id=1, source_target_pairs={{0,4},{4,8},{8,12},{1,5},{5,9},{9,13},{2,6},{6,10},{10,14},{3,7},{... | collective-permute-start | bytes 147464 | tf_op jit(solution)/shard_map/ppermute | solution.py:12
  303.3 8.1 %collective-permute-start.23 = (f32[1,2,2,3,6,1,128]{6,5,4,3,1,2,0:T(1,128)S(1)}, f32[1,2,2,3,6,1,128]{6,5,4,3,1,2,0:T(1,128)S(1)}, u32[]{:S(2)}, u32[]{:S(2)}) collective-permute-start(f32[1,2,2,3,6,1,128]{6,5,4,3,1,2,0:T(1,128)S(1)} %get-tuple-element.88), channel_id=1, source_target_pairs={{1,0},{2,1},{3,2},{5,4},{6,5},{7,6},{9,8},{10,9},{11,10},{13,12},{... | collective-permute-start | bytes 110600 | tf_op jit(solution)/shard_map/ppermute | solution.py:15
  307.6 5.9 %collective-permute-start.22 = (f32[1,2,2,3,6,1,128]{6,5,4,3,1,2,0:T(1,128)S(1)}, f32[1,2,2,3,6,1,128]{6,5,4,3,1,2,0:T(1,128)S(1)}, u32[]{:S(2)}, u32[]{:S(2)}) collective-permute-start(f32[1,2,2,3,6,1,128]{6,5,4,3,1,2,0:T(1,128)S(1)} %get-tuple-element.87), channel_id=1, source_target_pairs={{0,1},{1,2},{2,3},{4,5},{5,6},{6,7},{8,9},{9,10},{10,11},{12,13},{... | collective-permute-start | bytes 110600 | tf_op jit(solution)/shard_map/ppermute | solution.py:12
where the time goes:
time: 536 us; the launch traced here: 535 us
  blocking collectives  406 us (76%)
  starting transfers between devices  63.4 us (12%)
  waiting for transfers between devices  42.8 us (8%)
  other arithmetic  15.3 us (3%)
    psum x6, blocking collectives, inner_sums(): return lax.psum((dot_real, dot_imag, squares), ('gx', 'gy'))  225 us
    unnamed x1, blocking collectives  181 us
    ppermute x12, starting transfers between devices, extended_2(): lax.ppermute(lax.slice_in_dim(block, 0, width, axis=dim), axis, backward)  37.6 us
    ppermute x12, starting transfers between devices, extended_2(): lax.ppermute(lax.slice_in_dim(block, block.shape[dim] - width, None, axis...  25.8 us
    ppermute x12, waiting for transfers between devices, extended_2(): lax.ppermute(lax.slice_in_dim(block, block.shape[dim] - width, None, axis...  25.3 us
    ppermute x12, waiting for transfers between devices, extended_2(): lax.ppermute(lax.slice_in_dim(block, 0, width, axis=dim), axis, backward)  17.5 us
  transfers between devices with their start and end apart: 24, of which 17 were waited for; matrix products, arithmetic and copies ran while one was open for 2% of the time, Pallas kernels for 0%

commit v1 on v0

--- a/solution.py
+++ b/solution.py
@@ -84,7 +84,7 @@
     dot_real = jnp.sum(mapped_real * resid_real + mapped_imag * resid_imag, axis=axes_all)
     dot_imag = jnp.sum(mapped_real * resid_imag - mapped_imag * resid_real, axis=axes_all)
     squares = jnp.sum(mapped_real * mapped_real + mapped_imag * mapped_imag, axis=axes_all)
-    return lax.psum((dot_real, dot_imag, squares), ("gx", "gy"))
+    return lax.psum(lax.psum((dot_real, dot_imag, squares), "gy"), "gx")
 
 
 def complex_times(alpha_real, alpha_imag, fields):

time: 536 us -> 417 us (0.78)
  blocking collectives: 406 us -> 281 us
  starting transfers between devices: 63.4 us -> 70 us
    psum x6 -> x12, blocking collectives: 225 us -> 101 us  [inner_sums(): return lax.psum(lax.psum((dot_real, dot_imag, squares), 'gy'), 'gx')]
    ppermute x12, starting transfers between devices: 25.8 us -> 33.1 us  [extended_2(): lax.ppermute(lax.slice_in_dim(block, block.shape[dim] - width, None, axis...]
where the time goes in v1:
time: 417 us; the launch traced here: 416 us
  blocking collectives  281 us (67%)
  starting transfers between devices  70 us (17%)
  waiting for transfers between devices  42.9 us (10%)
  other arithmetic  15.3 us (4%)
  local copies, waits for them, and re-layouts  4.76 us (1%)
    unnamed x1, blocking collectives  180 us
    psum x12, blocking collectives, inner_sums(): return lax.psum(lax.psum((dot_real, dot_imag, squares), 'gy'), 'gx')  101 us
    ppermute x12, starting transfers between devices, extended_2(): lax.ppermute(lax.slice_in_dim(block, 0, width, axis=dim), axis, backward)  36.8 us
    ppermute x12, starting transfers between devices, extended_2(): lax.ppermute(lax.slice_in_dim(block, block.shape[dim] - width, None, axis...  33.1 us
    ppermute x12, waiting for transfers between devices, extended_2(): lax.ppermute(lax.slice_in_dim(block, block.shape[dim] - width, None, axis...  25.4 us
    ppermute x12, waiting for transfers between devices, extended_2(): lax.ppermute(lax.slice_in_dim(block, 0, width, axis=dim), axis, backward)  17.6 us
  transfers between devices with their start and end apart: 24, of which 17 were waited for; matrix products, arithmetic and copies ran while one was open for 2% of the time, Pallas kernels for 0%

profile of v1, /device:TPU:8, one launch (start us, length us, event | category | flops | bytes accessed | tf_op | source)
XLA Modules:
  0.0 416.2 jit_solution(13677537736230293020)
XLA Ops:
  2.9 4.5 %collective-permute-start = (f32[1,2,2,3,1,8,128]{6,5,4,3,1,2,0:T(8,128)S(1)}, f32[1,2,2,3,1,8,128]{6,5,4,3,1,2,0:T(8,128)S(1)}, u32[]{:S(2)}, u32[]{:S(2)}) collective-permute-start(f32[1,2,2,3,1,8,128]{6,5,4,3,1,2,0:T(8,128)S(1)} %get-tuple-element.162), channel_id=1, source_target_pairs={{0,4},{4,8},{8,12},{1,5},{5,9},{9,13},{2,6},{6,10},{10,14},{3,7},{... | collective-permute-start | bytes 147464 | tf_op jit(solution)/shard_map/ppermute | solution.py:12
  9.2 7.7 %collective-permute-start.3 = (f32[1,2,2,3,6,1,128]{6,5,4,3,1,2,0:T(1,128)S(1)}, f32[1,2,2,3,6,1,128]{6,5,4,3,1,2,0:T(1,128)S(1)}, u32[]{:S(2)}, u32[]{:S(2)}) collective-permute-start(f32[1,2,2,3,6,1,128]{6,5,4,3,1,2,0:T(1,128)S(1)} %get-tuple-element.116), channel_id=1, source_target_pairs={{1,0},{2,1},{3,2},{5,4},{6,5},{7,6},{9,8},{10,9},{11,10},{13,12},{... | collective-permute-start | bytes 110600 | tf_op jit(solution)/shard_map/ppermute | solution.py:15
  23.7 7.4 %all-reduce.30 = (f32[1,2]{1,0:T(1,128)S(1)}, f32[1,2]{1,0:T(1,128)S(1)}, f32[1,2]{1,0:T(1,128)S(1)}) all-reduce(f32[1,2]{1,0:T(1,128)S(1)} %bitcast.360, f32[1,2]{1,0:T(1,128)S(1)} %bitcast.359, f32[1,2]{1,0:T(1,128)S(1)} %bitcast.358), channel_id=1, replica_groups=mesh['af'=32,'gx'=4,'gy'=4] {'gy'}, use_global_device_ids=true, to_apply=%region_1.2 | all-reduce | flops 6 | bytes 48 | tf_op jit(solution)/shard_map/psum | solution.py:87
  31.1 10.7 %all-reduce.36 = (f32[1,2]{1,0:T(1,128)S(1)}, f32[1,2]{1,0:T(1,128)S(1)}, f32[1,2]{1,0:T(1,128)S(1)}) all-reduce(f32[1,2]{1,0:T(1,128)S(1)} %get-tuple-element.37, f32[1,2]{1,0:T(1,128)S(1)} %get-tuple-element.38, f32[1,2]{1,0:T(1,128)S(1)} %get-tuple-element.39), channel_id=1, replica_groups=mesh['af'=32,'gx'=4,'gy'=4] {'gx'}, use_global_device_ids=true, to_apply=%region_2.3 | all-reduce | flops 6 | bytes 48 | tf_op jit(solution)/shard_map/psum | solution.py:87
  46.0 4.2 %collective-permute-done.5 = f32[1,2,2,3,1,8,128]{6,5,4,1,2,3,0:T(8,128)S(1)} collective-permute-done((f32[1,2,2,3,1,8,128]{6,5,4,1,2,3,0:T(8,128)S(1)}, f32[1,2,2,3,1,8,128]{6,5,4,1,2,3,0:T(8,128)S(1)}, u32[]{:S(2)}, u32[]{:S(2)}) %collective-permute-start.5) | collective-permute-done | bytes 49184 | tf_op jit(solution)/shard_map/ppermute | solution.py:15
  50.3 4.2 %collective-permute-start.7 = (f32[1,2,2,3,6,1,128]{6,5,4,1,2,3,0:T(1,128)S(1)}, f32[1,2,2,3,6,1,128]{6,5,4,1,2,3,0:T(1,128)S(1)}, u32[]{:S(2)}, u32[]{:S(2)}) collective-permute-start(f32[1,2,2,3,6,1,128]{6,5,4,1,2,3,0:T(1,128)S(1)} %get-tuple-element.114), channel_id=1, source_target_pairs={{1,0},{2,1},{3,2},{5,4},{6,5},{7,6},{9,8},{10,9},{11,10},{13,12},{... | collective-permute-start | bytes 110600 | tf_op jit(solution)/shard_map/ppermute | solution.py:15
  56.4 3.9 collective-permute-done.6
  61.2 7.4 %all-reduce.29 = (f32[1,2]{1,0:T(1,128)S(1)}, f32[1,2]{1,0:T(1,128)S(1)}, f32[1,2]{1,0:T(1,128)S(1)}) all-reduce(f32[1,2]{1,0:T(1,128)S(1)} %bitcast.363, f32[1,2]{1,0:T(1,128)S(1)} %bitcast.362, f32[1,2]{1,0:T(1,128)S(1)} %bitcast.361), channel_id=1, replica_groups=mesh['af'=32,'gx'=4,'gy'=4] {'gy'}, use_global_device_ids=true, to_apply=%region_10.11 | all-reduce | flops 6 | bytes 48 | tf_op jit(solution)/shard_map/psum | solution.py:87
  68.6 9.0 %all-reduce.35 = (f32[1,2]{1,0:T(1,128)S(1)}, f32[1,2]{1,0:T(1,128)S(1)}, f32[1,2]{1,0:T(1,128)S(1)}) all-reduce(f32[1,2]{1,0:T(1,128)S(1)} %get-tuple-element.34, f32[1,2]{1,0:T(1,128)S(1)} %get-tuple-element.35, f32[1,2]{1,0:T(1,128)S(1)} %get-tuple-element.36), channel_id=1, replica_groups=mesh['af'=32,'gx'=4,'gy'=4] {'gx'}, use_global_device_ids=true, to_apply=%region_11.12 | all-reduce | flops 6 | bytes 48 | tf_op jit(solution)/shard_map/psum | solution.py:87
  81.8 6.1 %scatter_custom_fusion = f32[4096]{0:T(1024)S(1)} fusion(s32[1024]{0:T(1024)S(1)} %compare_select_fusion, f32[1024]{0:T(1024)} %bitcast.376, f32[]{:T(128)} %constant.59.clone.1), kind=kCustom, calls=%fused_computation.288 | custom fusion | flops 1024 | bytes 16896 | tf_op jit(solution)/shard_map/scatter-add | solution.py:124
  89.2 4.6 %collective-permute-done.9 = f32[1,2,2,3,1,8,128]{6,5,4,1,2,3,0:T(8,128)S(1)} collective-permute-done((f32[1,2,2,3,1,8,128]{6,5,4,1,2,3,0:T(8,128)S(1)}, f32[1,2,2,3,1,8,128]{6,5,4,1,2,3,0:T(8,128)S(1)}, u32[]{:S(2)}, u32[]{:S(2)}) %collective-permute-start.9) | collective-permute-done | bytes 49184 | tf_op jit(solution)/shard_map/ppermute | solution.py:15
  93.9 4.2 %collective-permute-start.11 = (f32[1,2,2,3,6,1,128]{6,5,4,1,2,3,0:T(1,128)S(1)}, f32[1,2,2,3,6,1,128]{6,5,4,1,2,3,0:T(1,128)S(1)}, u32[]{:S(2)}, u32[]{:S(2)}) collective-permute-start(f32[1,2,2,3,6,1,128]{6,5,4,1,2,3,0:T(1,128)S(1)} %get-tuple-element.112), channel_id=1, source_target_pairs={{1,0},{2,1},{3,2},{5,4},{6,5},{7,6},{9,8},{10,9},{11,10},{13,12},{... | collective-permute-start | bytes 110600 | tf_op jit(solution)/shard_map/ppermute | solution.py:15
  100.2 3.8 collective-permute-done.10
  104.9 7.4 %all-reduce.28 = (f32[1,2]{1,0:T(1,128)S(1)}, f32[1,2]{1,0:T(1,128)S(1)}, f32[1,2]{1,0:T(1,128)S(1)}) all-reduce(f32[1,2]{1,0:T(1,128)S(1)} %bitcast.366, f32[1,2]{1,0:T(1,128)S(1)} %bitcast.365, f32[1,2]{1,0:T(1,128)S(1)} %bitcast.364), channel_id=1, replica_groups=mesh['af'=32,'gx'=4,'gy'=4] {'gy'}, use_global_device_ids=true, to_apply=%region_19.20 | all-reduce | flops 6 | bytes 48 | tf_op jit(solution)/shard_map/psum | solution.py:87
  112.3 8.4 %all-reduce.34 = (f32[1,2]{1,0:T(1,128)S(1)}, f32[1,2]{1,0:T(1,128)S(1)}, f32[1,2]{1,0:T(1,128)S(1)}) all-reduce(f32[1,2]{1,0:T(1,128)S(1)} %get-tuple-element.31, f32[1,2]{1,0:T(1,128)S(1)} %get-tuple-element.32, f32[1,2]{1,0:T(1,128)S(1)} %get-tuple-element.33), channel_id=1, replica_groups=mesh['af'=32,'gx'=4,'gy'=4] {'gx'}, use_global_device_ids=true, to_apply=%region_20.21 | all-reduce | flops 6 | bytes 48 | tf_op jit(solution)/shard_map/psum | solution.py:87
  121.4 3.9 collective-permute-start.12
  127.1 4.3 %collective-permute-done.13 = f32[1,2,2,3,1,8,128]{6,5,4,1,2,3,0:T(8,128)S(1)} collective-permute-done((f32[1,2,2,3,1,8,128]{6,5,4,1,2,3,0:T(8,128)S(1)}, f32[1,2,2,3,1,8,128]{6,5,4,1,2,3,0:T(8,128)S(1)}, u32[]{:S(2)}, u32[]{:S(2)}) %collective-permute-start.13) | collective-permute-done | bytes 49184 | tf_op jit(solution)/shard_map/ppermute | solution.py:15
  131.4 4.2 %collective-permute-start.15 = (f32[1,2,2,3,6,1,128]{6,5,4,1,2,3,0:T(1,128)S(1)}, f32[1,2,2,3,6,1,128]{6,5,4,1,2,3,0:T(1,128)S(1)}, u32[]{:S(2)}, u32[]{:S(2)}) collective-permute-start(f32[1,2,2,3,6,1,128]{6,5,4,1,2,3,0:T(1,128)S(1)} %get-tuple-element.110), channel_id=1, source_target_pairs={{1,0},{2,1},{3,2},{5,4},{6,5},{7,6},{9,8},{10,9},{11,10},{13,12},{... | collective-permute-start | bytes 110600 | tf_op jit(solution)/shard_map/ppermute | solution.py:15
  137.6 3.9 collective-permute-done.14
  142.4 7.4 %all-reduce.27 = (f32[1,2]{1,0:T(1,128)S(1)}, f32[1,2]{1,0:T(1,128)S(1)}, f32[1,2]{1,0:T(1,128)S(1)}) all-reduce(f32[1,2]{1,0:T(1,128)S(1)} %bitcast.369, f32[1,2]{1,0:T(1,128)S(1)} %bitcast.368, f32[1,2]{1,0:T(1,128)S(1)} %bitcast.367), channel_id=1, replica_groups=mesh['af'=32,'gx'=4,'gy'=4] {'gy'}, use_global_device_ids=true, to_apply=%region_29.30 | all-reduce | flops 6 | bytes 48 | tf_op jit(solution)/shard_map/psum | solution.py:87
  149.8 8.4 %all-reduce.33 = (f32[1,2]{1,0:T(1,128)S(1)}, f32[1,2]{1,0:T(1,128)S(1)}, f32[1,2]{1,0:T(1,128)S(1)}) all-reduce(f32[1,2]{1,0:T(1,128)S(1)} %get-tuple-element.28, f32[1,2]{1,0:T(1,128)S(1)} %get-tuple-element.29, f32[1,2]{1,0:T(1,128)S(1)} %get-tuple-element.30), channel_id=1, replica_groups=mesh['af'=32,'gx'=4,'gy'=4] {'gx'}, use_global_device_ids=true, to_apply=%region_30.31 | all-reduce | flops 6 | bytes 48 | tf_op jit(solution)/shard_map/psum | solution.py:87
  159.0 3.9 collective-permute-start.16
  164.7 4.2 %collective-permute-done.17 = f32[1,2,2,3,1,8,128]{6,5,4,1,2,3,0:T(8,128)S(1)} collective-permute-done((f32[1,2,2,3,1,8,128]{6,5,4,1,2,3,0:T(8,128)S(1)}, f32[1,2,2,3,1,8,128]{6,5,4,1,2,3,0:T(8,128)S(1)}, u32[]{:S(2)}, u32[]{:S(2)}) %collective-permute-start.17) | collective-permute-done | bytes 49184 | tf_op jit(solution)/shard_map/ppermute | solution.py:15
  168.9 4.2 %collective-permute-start.19 = (f32[1,2,2,3,6,1,128]{6,5,4,1,2,3,0:T(1,128)S(1)}, f32[1,2,2,3,6,1,128]{6,5,4,1,2,3,0:T(1,128)S(1)}, u32[]{:S(2)}, u32[]{:S(2)}) collective-permute-start(f32[1,2,2,3,6,1,128]{6,5,4,1,2,3,0:T(1,128)S(1)} %get-tuple-element.108), channel_id=1, source_target_pairs={{1,0},{2,1},{3,2},{5,4},{6,5},{7,6},{9,8},{10,9},{11,10},{13,12},{... | collective-permute-start | bytes 110600 | tf_op jit(solution)/shard_map/ppermute | solution.py:15
  175.1 3.9 collective-permute-done.18
  179.9 7.4 %all-reduce.26 = (f32[1,2]{1,0:T(1,128)S(1)}, f32[1,2]{1,0:T(1,128)S(1)}, f32[1,2]{1,0:T(1,128)S(1)}) all-reduce(f32[1,2]{1,0:T(1,128)S(1)} %bitcast.372, f32[1,2]{1,0:T(1,128)S(1)} %bitcast.371, f32[1,2]{1,0:T(1,128)S(1)} %bitcast.370), channel_id=1, replica_groups=mesh['af'=32,'gx'=4,'gy'=4] {'gy'}, use_global_device_ids=true, to_apply=%region_38.39 | all-reduce | flops 6 | bytes 48 | tf_op jit(solution)/shard_map/psum | solution.py:87
  187.3 9.0 %all-reduce.32 = (f32[1,2]{1,0:T(1,128)S(1)}, f32[1,2]{1,0:T(1,128)S(1)}, f32[1,2]{1,0:T(1,128)S(1)}) all-reduce(f32[1,2]{1,0:T(1,128)S(1)} %get-tuple-element.25, f32[1,2]{1,0:T(1,128)S(1)} %get-tuple-element.26, f32[1,2]{1,0:T(1,128)S(1)} %get-tuple-element.27), channel_id=1, replica_groups=mesh['af'=32,'gx'=4,'gy'=4] {'gx'}, use_global_device_ids=true, to_apply=%region_39.40 | all-reduce | flops 6 | bytes 48 | tf_op jit(solution)/shard_map/psum | solution.py:87
  198.5 4.5 %collective-permute-start.20 = (f32[1,2,2,3,1,8,128]{6,5,4,3,1,2,0:T(8,128)S(1)}, f32[1,2,2,3,1,8,128]{6,5,4,3,1,2,0:T(8,128)S(1)}, u32[]{:S(2)}, u32[]{:S(2)}) collective-permute-start(f32[1,2,2,3,1,8,128]{6,5,4,3,1,2,0:T(8,128)S(1)} %get-tuple-element.134), channel_id=1, source_target_pairs={{0,4},{4,8},{8,12},{1,5},{5,9},{9,13},{2,6},{6,10},{10,14},{3,7},{... | collective-permute-start | bytes 147464 | tf_op jit(solution)/shard_map/ppermute | solution.py:12
  204.8 4.4 %collective-permute-start.23 = (f32[1,2,2,3,6,1,128]{6,5,4,3,1,2,0:T(1,128)S(1)}, f32[1,2,2,3,6,1,128]{6,5,4,3,1,2,0:T(1,128)S(1)}, u32[]{:S(2)}, u32[]{:S(2)}) collective-permute-start(f32[1,2,2,3,6,1,128]{6,5,4,3,1,2,0:T(1,128)S(1)} %get-tuple-element.106), channel_id=1, source_target_pairs={{1,0},{2,1},{3,2},{5,4},{6,5},{7,6},{9,8},{10,9},{11,10},{13,12},{... | collective-permute-start | bytes 110600 | tf_op jit(solution)/shard_map/ppermute | solution.py:15
  216.0 7.6 %all-reduce.25 = (f32[1,2]{1,0:T(1,128)S(1)}, f32[1,2]{1,0:T(1,128)S(1)}, f32[1,2]{1,0:T(1,128)S(1)}) all-reduce(f32[1,2]{1,0:T(1,128)S(1)} %bitcast.373, f32[1,2]{1,0:T(1,128)S(1)} %bitcast.375, f32[1,2]{1,0:T(1,128)S(1)} %bitcast.374), channel_id=1, replica_groups=mesh['af'=32,'gx'=4,'gy'=4] {'gy'}, use_global_device_ids=true, to_apply=%region_47.48 | all-reduce | flops 6 | bytes 48 | tf_op jit(solution)/shard_map/psum | solution.py:87
  223.7 10.7 %all-reduce.31 = (f32[1,2]{1,0:T(1,128)S(1)}, f32[1,2]{1,0:T(1,128)S(1)}, f32[1,2]{1,0:T(1,128)S(1)}) all-reduce(f32[1,2]{1,0:T(1,128)S(1)} %get-tuple-element.22, f32[1,2]{1,0:T(1,128)S(1)} %get-tuple-element.23, f32[1,2]{1,0:T(1,128)S(1)} %get-tuple-element.24), channel_id=1, replica_groups=mesh['af'=32,'gx'=4,'gy'=4] {'gx'}, use_global_device_ids=true, to_apply=%region_48.49 | all-reduce | flops 6 | bytes 48 | tf_op jit(solution)/shard_map/psum | solution.py:87
  235.6 180.0 %all-reduce.24 = f32[3,4,8,128]{2,3,1,0:T(8,128)S(1)} all-reduce(f32[3,4,8,128]{2,3,1,0:T(8,128)S(1)} %copy.127), channel_id=2, replica_groups=mesh['af'=32,'gx'=4,'gy'=4] {'af'}, use_global_device_ids=true, to_apply=%region_56.57.clone | all-reduce | flops 12288 | bytes 98304
  (170 shorter events, 48.1 us)
Async XLA Ops:
  0.0 1.5 copy-start
  1.6 6.0 %collective-permute-start.1 = (f32[1,2,2,3,1,8,128]{6,5,4,3,1,2,0:T(8,128)S(1)}, f32[1,2,2,3,1,8,128]{6,5,4,3,1,2,0:T(8,128)S(1)}, u32[]{:S(2)}, u32[]{:S(2)}) collective-permute-start(f32[1,2,2,3,1,8,128]{6,5,4,3,1,2,0:T(8,128)S(1)} %get-tuple-element.163), channel_id=1, source_target_pairs={{4,0},{8,4},{12,8},{5,1},{9,5},{13,9},{6,2},{10,6},{14,10},{7,3},{... | collective-permute-start | bytes 147464 | tf_op jit(solution)/shard_map/ppermute | solution.py:15
  2.9 6.3 %collective-permute-start = (f32[1,2,2,3,1,8,128]{6,5,4,3,1,2,0:T(8,128)S(1)}, f32[1,2,2,3,1,8,128]{6,5,4,3,1,2,0:T(8,128)S(1)}, u32[]{:S(2)}, u32[]{:S(2)}) collective-permute-start(f32[1,2,2,3,1,8,128]{6,5,4,3,1,2,0:T(8,128)S(1)} %get-tuple-element.162), channel_id=1, source_target_pairs={{0,4},{4,8},{8,12},{1,5},{5,9},{9,13},{2,6},{6,10},{10,14},{3,7},{... | collective-permute-start | bytes 147464 | tf_op jit(solution)/shard_map/ppermute | solution.py:12
  9.2 9.7 %copy-start.1 = (f32[2,3]{1,0:T(2,128)S(1)}, f32[2,3]{1,0:T(2,128)}, u32[]{:S(2)}) copy-start(f32[2,3]{1,0:T(2,128)} %param.12) | copy-start | bytes 76
  9.2 10.4 %collective-permute-start.3 = (f32[1,2,2,3,6,1,128]{6,5,4,3,1,2,0:T(1,128)S(1)}, f32[1,2,2,3,6,1,128]{6,5,4,3,1,2,0:T(1,128)S(1)}, u32[]{:S(2)}, u32[]{:S(2)}) collective-permute-start(f32[1,2,2,3,6,1,128]{6,5,4,3,1,2,0:T(1,128)S(1)} %get-tuple-element.116), channel_id=1, source_target_pairs={{1,0},{2,1},{3,2},{5,4},{6,5},{7,6},{9,8},{10,9},{11,10},{13,12},{... | collective-permute-start | bytes 110600 | tf_op jit(solution)/shard_map/ppermute | solution.py:15
  17.0 5.9 %collective-permute-start.2 = (f32[1,2,2,3,6,1,128]{6,5,4,3,1,2,0:T(1,128)S(1)}, f32[1,2,2,3,6,1,128]{6,5,4,3,1,2,0:T(1,128)S(1)}, u32[]{:S(2)}, u32[]{:S(2)}) collective-permute-start(f32[1,2,2,3,6,1,128]{6,5,4,3,1,2,0:T(1,128)S(1)} %get-tuple-element.115), channel_id=1, source_target_pairs={{0,1},{1,2},{2,3},{4,5},{5,6},{6,7},{8,9},{9,10},{10,11},{12,13},{... | collective-permute-start | bytes 110600 | tf_op jit(solution)/shard_map/ppermute | solution.py:12
  42.7 3.3 collective-permute-start.4
  44.2 6.0 %collective-permute-start.5 = (f32[1,2,2,3,1,8,128]{6,5,4,1,2,3,0:T(8,128)S(1)}, f32[1,2,2,3,1,8,128]{6,5,4,1,2,3,0:T(8,128)S(1)}, u32[]{:S(2)}, u32[]{:S(2)}) collective-permute-start(f32[1,2,2,3,1,8,128]{6,5,4,1,2,3,0:T(8,128)S(1)} %copy.178), channel_id=1, source_target_pairs={{4,0},{8,4},{12,8},{5,1},{9,5},{13,9},{6,2},{10,6},{14,10},{7,3},{... | collective-permute-start | bytes 147464 | tf_op jit(solution)/shard_map/ppermute | solution.py:15
  50.3 6.2 %collective-permute-start.7 = (f32[1,2,2,3,6,1,128]{6,5,4,1,2,3,0:T(1,128)S(1)}, f32[1,2,2,3,6,1,128]{6,5,4,1,2,3,0:T(1,128)S(1)}, u32[]{:S(2)}, u32[]{:S(2)}) collective-permute-start(f32[1,2,2,3,6,1,128]{6,5,4,1,2,3,0:T(1,128)S(1)} %get-tuple-element.114), channel_id=1, source_target_pairs={{1,0},{2,1},{3,2},{5,4},{6,5},{7,6},{9,8},{10,9},{11,10},{13,12},{... | collective-permute-start | bytes 110600 | tf_op jit(solution)/shard_map/ppermute | solution.py:15
  54.5 5.9 %collective-permute-start.6 = (f32[1,2,2,3,6,1,128]{6,5,4,1,2,3,0:T(1,128)S(1)}, f32[1,2,2,3,6,1,128]{6,5,4,1,2,3,0:T(1,128)S(1)}, u32[]{:S(2)}, u32[]{:S(2)}) collective-permute-start(f32[1,2,2,3,6,1,128]{6,5,4,1,2,3,0:T(1,128)S(1)} %get-tuple-element.113), channel_id=1, source_target_pairs={{0,1},{1,2},{2,3},{4,5},{5,6},{6,7},{8,9},{9,10},{10,11},{12,13},{... | collective-permute-start | bytes 110600 | tf_op jit(solution)/shard_map/ppermute | solution.py:12
  78.4 3.3 copy-start.2
  78.5 10.7 %collective-permute-start.8 = (f32[1,2,2,3,1,8,128]{6,5,4,1,2,3,0:T(8,128)S(1)}, f32[1,2,2,3,1,8,128]{6,5,4,1,2,3,0:T(8,128)S(1)}, u32[]{:S(2)}, u32[]{:S(2)}) collective-permute-start(f32[1,2,2,3,1,8,128]{6,5,4,1,2,3,0:T(8,128)S(1)} %copy.179), channel_id=1, source_target_pairs={{0,4},{4,8},{8,12},{1,5},{5,9},{9,13},{2,6},{6,10},{10,14},{3,7},{... | collective-permute-start | bytes 147464 | tf_op jit(solution)/shard_map/ppermute | solution.py:12
  87.9 6.0 %collective-permute-start.9 = (f32[1,2,2,3,1,8,128]{6,5,4,1,2,3,0:T(8,128)S(1)}, f32[1,2,2,3,1,8,128]{6,5,4,1,2,3,0:T(8,128)S(1)}, u32[]{:S(2)}, u32[]{:S(2)}) collective-permute-start(f32[1,2,2,3,1,8,128]{6,5,4,1,2,3,0:T(8,128)S(1)} %copy.180), channel_id=1, source_target_pairs={{4,0},{8,4},{12,8},{5,1},{9,5},{13,9},{6,2},{10,6},{14,10},{7,3},{... | collective-permute-start | bytes 147464 | tf_op jit(solution)/shard_map/ppermute | solution.py:15
  93.9 6.3 %collective-permute-start.11 = (f32[1,2,2,3,6,1,128]{6,5,4,1,2,3,0:T(1,128)S(1)}, f32[1,2,2,3,6,1,128]{6,5,4,1,2,3,0:T(1,128)S(1)}, u32[]{:S(2)}, u32[]{:S(2)}) collective-permute-start(f32[1,2,2,3,6,1,128]{6,5,4,1,2,3,0:T(1,128)S(1)} %get-tuple-element.112), channel_id=1, source_target_pairs={{1,0},{2,1},{3,2},{5,4},{6,5},{7,6},{9,8},{10,9},{11,10},{13,12},{... | collective-permute-start | bytes 110600 | tf_op jit(solution)/shard_map/ppermute | solution.py:15
  98.2 1.9 copy-start.3
  98.2 5.9 %collective-permute-start.10 = (f32[1,2,2,3,6,1,128]{6,5,4,1,2,3,0:T(1,128)S(1)}, f32[1,2,2,3,6,1,128]{6,5,4,1,2,3,0:T(1,128)S(1)}, u32[]{:S(2)}, u32[]{:S(2)}) collective-permute-start(f32[1,2,2,3,6,1,128]{6,5,4,1,2,3,0:T(1,128)S(1)} %get-tuple-element.111), channel_id=1, source_target_pairs={{0,1},{1,2},{2,3},{4,5},{5,6},{6,7},{8,9},{9,10},{10,11},{12,13},{... | collective-permute-start | bytes 110600 | tf_op jit(solution)/shard_map/ppermute | solution.py:12
  121.4 5.6 %collective-permute-start.12 = (f32[1,2,2,3,1,8,128]{6,5,4,1,2,3,0:T(8,128)S(1)}, f32[1,2,2,3,1,8,128]{6,5,4,1,2,3,0:T(8,128)S(1)}, u32[]{:S(2)}, u32[]{:S(2)}) collective-permute-start(f32[1,2,2,3,1,8,128]{6,5,4,1,2,3,0:T(8,128)S(1)} %copy.181), channel_id=1, source_target_pairs={{0,4},{4,8},{8,12},{1,5},{5,9},{9,13},{2,6},{6,10},{10,14},{3,7},{... | collective-permute-start | bytes 147464 | tf_op jit(solution)/shard_map/ppermute | solution.py:12
  125.3 6.0 %collective-permute-start.13 = (f32[1,2,2,3,1,8,128]{6,5,4,1,2,3,0:T(8,128)S(1)}, f32[1,2,2,3,1,8,128]{6,5,4,1,2,3,0:T(8,128)S(1)}, u32[]{:S(2)}, u32[]{:S(2)}) collective-permute-start(f32[1,2,2,3,1,8,128]{6,5,4,1,2,3,0:T(8,128)S(1)} %copy.182), channel_id=1, source_target_pairs={{4,0},{8,4},{12,8},{5,1},{9,5},{13,9},{6,2},{10,6},{14,10},{7,3},{... | collective-permute-start | bytes 147464 | tf_op jit(solution)/shard_map/ppermute | solution.py:15
  131.4 6.2 %collective-permute-start.15 = (f32[1,2,2,3,6,1,128]{6,5,4,1,2,3,0:T(1,128)S(1)}, f32[1,2,2,3,6,1,128]{6,5,4,1,2,3,0:T(1,128)S(1)}, u32[]{:S(2)}, u32[]{:S(2)}) collective-permute-start(f32[1,2,2,3,6,1,128]{6,5,4,1,2,3,0:T(1,128)S(1)} %get-tuple-element.110), channel_id=1, source_target_pairs={{1,0},{2,1},{3,2},{5,4},{6,5},{7,6},{9,8},{10,9},{11,10},{13,12},{... | collective-permute-start | bytes 110600 | tf_op jit(solution)/shard_map/ppermute | solution.py:15
  135.7 5.9 %collective-permute-start.14 = (f32[1,2,2,3,6,1,128]{6,5,4,1,2,3,0:T(1,128)S(1)}, f32[1,2,2,3,6,1,128]{6,5,4,1,2,3,0:T(1,128)S(1)}, u32[]{:S(2)}, u32[]{:S(2)}) collective-permute-start(f32[1,2,2,3,6,1,128]{6,5,4,1,2,3,0:T(1,128)S(1)} %get-tuple-element.109), channel_id=1, source_target_pairs={{0,1},{1,2},{2,3},{4,5},{5,6},{6,7},{8,9},{9,10},{10,11},{12,13},{... | collective-permute-start | bytes 110600 | tf_op jit(solution)/shard_map/ppermute | solution.py:12
  159.0 5.6 %collective-permute-start.16 = (f32[1,2,2,3,1,8,128]{6,5,4,1,2,3,0:T(8,128)S(1)}, f32[1,2,2,3,1,8,128]{6,5,4,1,2,3,0:T(8,128)S(1)}, u32[]{:S(2)}, u32[]{:S(2)}) collective-permute-start(f32[1,2,2,3,1,8,128]{6,5,4,1,2,3,0:T(8,128)S(1)} %copy.183), channel_id=1, source_target_pairs={{0,4},{4,8},{8,12},{1,5},{5,9},{9,13},{2,6},{6,10},{10,14},{3,7},{... | collective-permute-start | bytes 147464 | tf_op jit(solution)/shard_map/ppermute | solution.py:12
  162.9 6.0 %collective-permute-start.17 = (f32[1,2,2,3,1,8,128]{6,5,4,1,2,3,0:T(8,128)S(1)}, f32[1,2,2,3,1,8,128]{6,5,4,1,2,3,0:T(8,128)S(1)}, u32[]{:S(2)}, u32[]{:S(2)}) collective-permute-start(f32[1,2,2,3,1,8,128]{6,5,4,1,2,3,0:T(8,128)S(1)} %copy.184), channel_id=1, source_target_pairs={{4,0},{8,4},{12,8},{5,1},{9,5},{13,9},{6,2},{10,6},{14,10},{7,3},{... | collective-permute-start | bytes 147464 | tf_op jit(solution)/shard_map/ppermute | solution.py:15
  168.9 6.2 %collective-permute-start.19 = (f32[1,2,2,3,6,1,128]{6,5,4,1,2,3,0:T(1,128)S(1)}, f32[1,2,2,3,6,1,128]{6,5,4,1,2,3,0:T(1,128)S(1)}, u32[]{:S(2)}, u32[]{:S(2)}) collective-permute-start(f32[1,2,2,3,6,1,128]{6,5,4,1,2,3,0:T(1,128)S(1)} %get-tuple-element.108), channel_id=1, source_target_pairs={{1,0},{2,1},{3,2},{5,4},{6,5},{7,6},{9,8},{10,9},{11,10},{13,12},{... | collective-permute-start | bytes 110600 | tf_op jit(solution)/shard_map/ppermute | solution.py:15
  173.2 5.9 %collective-permute-start.18 = (f32[1,2,2,3,6,1,128]{6,5,4,1,2,3,0:T(1,128)S(1)}, f32[1,2,2,3,6,1,128]{6,5,4,1,2,3,0:T(1,128)S(1)}, u32[]{:S(2)}, u32[]{:S(2)}) collective-permute-start(f32[1,2,2,3,6,1,128]{6,5,4,1,2,3,0:T(1,128)S(1)} %get-tuple-element.107), channel_id=1, source_target_pairs={{0,1},{1,2},{2,3},{4,5},{5,6},{6,7},{8,9},{9,10},{10,11},{12,13},{... | collective-permute-start | bytes 110600 | tf_op jit(solution)/shard_map/ppermute | solution.py:12
  197.2 6.0 %collective-permute-start.21 = (f32[1,2,2,3,1,8,128]{6,5,4,3,1,2,0:T(8,128)S(1)}, f32[1,2,2,3,1,8,128]{6,5,4,3,1,2,0:T(8,128)S(1)}, u32[]{:S(2)}, u32[]{:S(2)}) collective-permute-start(f32[1,2,2,3,1,8,128]{6,5,4,3,1,2,0:T(8,128)S(1)} %get-tuple-element.135), channel_id=1, source_target_pairs={{4,0},{8,4},{12,8},{5,1},{9,5},{13,9},{6,2},{10,6},{14,10},{7,3},{... | collective-permute-start | bytes 147464 | tf_op jit(solution)/shard_map/ppermute | solution.py:15
  198.5 6.3 %collective-permute-start.20 = (f32[1,2,2,3,1,8,128]{6,5,4,3,1,2,0:T(8,128)S(1)}, f32[1,2,2,3,1,8,128]{6,5,4,3,1,2,0:T(8,128)S(1)}, u32[]{:S(2)}, u32[]{:S(2)}) collective-permute-start(f32[1,2,2,3,1,8,128]{6,5,4,3,1,2,0:T(8,128)S(1)} %get-tuple-element.134), channel_id=1, source_target_pairs={{0,4},{4,8},{8,12},{1,5},{5,9},{9,13},{2,6},{6,10},{10,14},{3,7},{... | collective-permute-start | bytes 147464 | tf_op jit(solution)/shard_map/ppermute | solution.py:12
  204.8 8.2 %collective-permute-start.23 = (f32[1,2,2,3,6,1,128]{6,5,4,3,1,2,0:T(1,128)S(1)}, f32[1,2,2,3,6,1,128]{6,5,4,3,1,2,0:T(1,128)S(1)}, u32[]{:S(2)}, u32[]{:S(2)}) collective-permute-start(f32[1,2,2,3,6,1,128]{6,5,4,3,1,2,0:T(1,128)S(1)} %get-tuple-element.106), channel_id=1, source_target_pairs={{1,0},{2,1},{3,2},{5,4},{6,5},{7,6},{9,8},{10,9},{11,10},{13,12},{... | collective-permute-start | bytes 110600 | tf_op jit(solution)/shard_map/ppermute | solution.py:15
  209.2 5.9 %collective-permute-start.22 = (f32[1,2,2,3,6,1,128]{6,5,4,3,1,2,0:T(1,128)S(1)}, f32[1,2,2,3,6,1,128]{6,5,4,3,1,2,0:T(1,128)S(1)}, u32[]{:S(2)}, u32[]{:S(2)}) collective-permute-start(f32[1,2,2,3,6,1,128]{6,5,4,3,1,2,0:T(1,128)S(1)} %get-tuple-element.105), channel_id=1, source_target_pairs={{0,1},{1,2},{2,3},{4,5},{5,6},{6,7},{8,9},{9,10},{10,11},{12,13},{... | collective-permute-start | bytes 110600 | tf_op jit(solution)/shard_map/ppermute | solution.py:12
